TPU v7x, 32 devices: a whole 2x2x4 slice. The times are simulated.
32 devices in a mesh: tm: 8 (over z, x), rows: 4 (over y, core).
Axes of the slice: x: 2, y: 2, z: 4, core: 2. Of those that a mesh axis runs over, the one named last changes fastest.
Arguments:
- features: bfloat16 [16, 4, 160, 512], P('tm', 'rows'), may hold values from -25 to 25
- norm_gain: float32 [512], replicated, may hold values from 0.1 to 1.9
- norm_bias: float32 [512], replicated, may hold values from -1 to 1
- weight: bfloat16 [3, 3, 3, 512, 256], replicated, may hold values from -0.0546875 to 0.0546875
- upstream: bfloat16 [16, 4, 160, 256], P('tm', 'rows'), may hold values from -20 to 20
Outputs:
- grad_features: bfloat16 [16, 4, 160, 512], P('tm', 'rows')
- grad_weight: float32 [3, 3, 3, 512, 256], P(None, None, None, 'tm', 'rows')
- grad_gain: float32 [512], replicated
- grad_bias: float32 [512], replicated
All inputs are finite; a program needn't handle non-finite values.
Results may differ from a plain program's by a relative error of at most 0.0015.
Values may be sent and summed in bfloat16 or wider, within the bound.
A program may use at most 64 MiB of HBM per device.

v0:
```python
import jax
import jax.numpy as jnp
from jax import lax
from jax.sharding import PartitionSpec as P

GROUPS = 32
CLIPS = 1


epsilon = 1e-06


def from_behind(value, axis, steps):
    count = lax.axis_size(axis)
    initial, last = (max(0, -steps), min(count, count - steps))
    return lax.ppermute(value, axis, [(source, source + steps) for source in range(initial, last)])


def padded(cells, sides, width):
    for axis, dim in sides:
        count = lax.axis_size(axis)
        ends = count - 1
        head = lax.slice_in_dim(cells, 0, width, axis=dim)
        tail = lax.slice_in_dim(cells, cells.shape[dim] - width, cells.shape[dim], axis=dim)
        cells = jnp.concatenate(
            [
                lax.ppermute(tail, axis, [(i, (i + 1) % count) for i in range(ends)]),
                cells,
                lax.ppermute(head, axis, [((i + 1) % count, i) for i in range(ends)]),
            ],
            axis=dim,
        )
    return cells


def on_device(features, norm_gain, norm_bias, weight, upstream):
    frames_dev, rows_dev, cols, chans = features.shape
    outs = upstream.shape[3]
    group_size = chans // GROUPS
    per_clip = lax.axis_size("tm") // CLIPS
    time_index = lax.axis_index("tm")
    clip_index = time_index // per_clip
    first_dev = time_index % per_clip == 0
    last_dev = time_index % per_clip == per_clip - 1
    selector = (jnp.arange(CLIPS) == clip_index).astype(jnp.float32)
    count_clip = frames_dev * rows_dev * cols * group_size * per_clip * lax.axis_size("rows")
    floats = features.astype(jnp.float32)
    grouped = floats.reshape(frames_dev, rows_dev, cols, GROUPS, group_size)
    local_sum = jnp.sum(grouped, axis=(0, 1, 2, 4))
    local_sq = jnp.sum(grouped * grouped, axis=(0, 1, 2, 4))
    total_sum, total_sq = lax.psum(
        (selector[:, None] * local_sum, selector[:, None] * local_sq), ("tm", "rows")
    )
    centre_val = jnp.sum(selector[:, None] * total_sum, axis=0) / count_clip
    spread = jnp.sum(selector[:, None] * total_sq, axis=0) / count_clip - centre_val * centre_val
    diffs = grouped - centre_val[:, None]
    inverse = lax.rsqrt(spread + epsilon)
    normed = (diffs * inverse[:, None]).reshape(frames_dev, rows_dev, cols, chans)
    preact = normed * norm_gain + norm_bias
    sig_val = jax.nn.sigmoid(preact)
    hidden = (preact * sig_val).astype(jnp.bfloat16)
    earlier = from_behind(hidden, "tm", 1)
    earlier = jnp.where(first_dev, jnp.concatenate([hidden[:1], hidden[:1]], axis=0), earlier)
    extended = jnp.concatenate([earlier, hidden], axis=0)
    extended = padded(extended, (("rows", 1),), 1)
    extended = jnp.pad(extended, ((0, 0), (0, 0), (1, 1), (0, 0)))
    up_flat = upstream.reshape(-1, outs)
    grad_taps = []
    for time_tap in range(3):
        for row_tap in range(3):
            for col_tap in range(3):
                slab = extended[
                    time_tap : time_tap + frames_dev,
                    row_tap : row_tap + rows_dev,
                    col_tap : col_tap + cols,
                ].reshape(-1, chans)
                grad_taps.append(
                    lax.dot_general(
                        slab, up_flat, (((0,), (0,)), ((), ())), preferred_element_type=jnp.float32
                    )
                )
    local_grad = jnp.stack(grad_taps).reshape(3, 3, 3, chans, outs)
    halfway = lax.psum_scatter(local_grad, "tm", scatter_dimension=3, tiled=True)
    grad_weight = lax.psum_scatter(halfway, "rows", scatter_dimension=4, tiled=True)
    later = from_behind(upstream, "tm", -1)
    later = jnp.where(last_dev, jnp.zeros_like(later), later)
    up_ext = jnp.concatenate([upstream, later], axis=0)
    up_ext = padded(up_ext, (("rows", 1),), 1)
    up_ext = jnp.pad(up_ext, ((0, 0), (0, 0), (1, 1), (0, 0)))
    dense = jnp.zeros((frames_dev * rows_dev * cols, chans), jnp.float32)
    for time_tap in range(3):
        for row_tap in range(3):
            for col_tap in range(3):
                slab = up_ext[
                    2 - time_tap : 2 - time_tap + frames_dev,
                    2 - row_tap : 2 - row_tap + rows_dev,
                    2 - col_tap : 2 - col_tap + cols,
                ].reshape(-1, outs)
                dense = dense + jnp.dot(
                    slab, weight[time_tap, row_tap, col_tap].T, preferred_element_type=jnp.float32
                )
    dense = dense.reshape(frames_dev, rows_dev, cols, chans)

    def pad_terms(unused):
        total = jnp.zeros((rows_dev * cols, chans), jnp.float32)
        for row_tap in range(3):
            for col_tap in range(3):
                first_slab = up_ext[
                    0, 2 - row_tap : 2 - row_tap + rows_dev, 2 - col_tap : 2 - col_tap + cols
                ].reshape(-1, outs)
                second_slab = up_ext[
                    1, 2 - row_tap : 2 - row_tap + rows_dev, 2 - col_tap : 2 - col_tap + cols
                ].reshape(-1, outs)
                total = total + jnp.dot(
                    first_slab, weight[0, row_tap, col_tap].T, preferred_element_type=jnp.float32
                )
                total = total + jnp.dot(
                    first_slab, weight[1, row_tap, col_tap].T, preferred_element_type=jnp.float32
                )
                total = total + jnp.dot(
                    second_slab, weight[0, row_tap, col_tap].T, preferred_element_type=jnp.float32
                )
        return total.reshape(rows_dev, cols, chans)

    def skip_terms(unused):
        return jnp.zeros((rows_dev, cols, chans), jnp.float32)

    extra = lax.cond(first_dev, pad_terms, skip_terms, 0)
    grad_hidden = dense.at[0].add(extra)
    grad_act = grad_hidden * sig_val * (1.0 + preact * (1.0 - sig_val))
    local_gain = jnp.sum(grad_act * normed, axis=(0, 1, 2))
    local_bias = jnp.sum(grad_act, axis=(0, 1, 2))
    clip_gain, clip_bias = lax.psum(
        (selector[:, None] * local_gain, selector[:, None] * local_bias), ("tm", "rows")
    )
    grad_gain = jnp.sum(clip_gain, axis=0)
    grad_bias = jnp.sum(clip_bias, axis=0)
    own_gain = jnp.sum(selector[:, None] * clip_gain, axis=0)
    own_bias = jnp.sum(selector[:, None] * clip_bias, axis=0)
    first_term = jnp.repeat(
        jnp.sum((norm_gain * own_bias).reshape(GROUPS, -1), axis=1) / count_clip, group_size
    )
    second_term = jnp.repeat(
        jnp.sum((norm_gain * own_gain).reshape(GROUPS, -1), axis=1) / count_clip, group_size
    )
    inverse_chan = jnp.repeat(inverse, group_size)
    grad_features = (
        inverse_chan * (grad_act * norm_gain - first_term - normed * second_term)
    ).astype(jnp.bfloat16)
    return (grad_features, grad_weight, grad_gain, grad_bias)


def solution(mesh):
    in_specs = (P("tm", "rows", None, None), P(), P(), P(), P("tm", "rows", None, None))
    out_specs = (P("tm", "rows", None, None), P(None, None, None, "tm", "rows"), P(), P())
    return jax.shard_map(
        on_device, mesh=mesh, in_specs=in_specs, out_specs=out_specs, check_vma=False
    )
```

profile of v0, /device:TPU:0, one launch (start us, length us, event | category | flops | bytes accessed | tf_op | source)
XLA Modules:
  0.0 425.4 jit_solution(6845196313905817065)
XLA Ops:
  7.2 1.3 collective-permute-start
  8.5 1.1 fusion.151
  10.0 43.2 %all-reduce.3 = (f32[1,32]{1,0:T(1,128)S(1)}, f32[1,32]{1,0:T(1,128)S(1)}) all-reduce(f32[1,32]{1,0:T(1,128)S(1)} %multiply_bitcast_fusion.1, f32[1,32]{1,0:T(1,128)S(1)} %multiply_bitcast_fusion.2), channel_id=1, replica_groups=mesh['tm'=8,'rows'=4] {'tm','rows'}, use_global_device_ids=true, to_apply=%region_5.6 | all-reduce | flops 64 | bytes 512 | tf_op jit(solution)/shard_map/psum | solution.py:51
  53.4 0.9 pad_maximum_fusion.1
  54.4 1.3 collective-permute-start.2
  55.7 3.1 collective-permute-start.1
  58.9 1.1 fusion.240
  60.0 1.4 select_maximum_fusion.2
  69.9 6.6 %conditional.1 = (f32[1,1,160,512]{3,2,1,0:T(8,128)S(1)}) conditional(s32[]{:T(128)} %convert_element_type.24, () %tuple.20, (bf16[4,3,162,256]{3,2,1,0:T(8,128)(2,1)S(1)}, bf16[3,3,3,512,256]{4,3,2,1,0:T(8,128)(2,1)S(1)}) %tuple.59), branch_computations={%region_6.7_spmd, %region_7.8_spmd} | conditional | flops 1134592000 | bytes 26656776 | solution.py:128
  77.0 1.3 collective-permute-start.3
  78.3 4.5 %collective-permute-done.3 = bf16[2,1,160,512]{3,2,0,1:T(8,128)(2,1)S(1)} collective-permute-done((bf16[2,1,160,512]{3,2,0,1:T(8,128)(2,1)S(1)}, bf16[2,1,160,512]{3,2,0,1:T(8,128)(2,1)S(1)}, u32[]{:S(2)}, u32[]{:S(2)}) %collective-permute-start.3) | collective-permute-done | bytes 327712 | tf_op jit(solution)/shard_map/ppermute | solution.py:16
  83.0 1.3 collective-permute-start.5
  84.3 6.4 %collective-permute-start.4 = (bf16[4,1,160,512]{3,2,0,1:T(8,128)(2,1)S(1)}, bf16[4,1,160,512]{3,2,0,1:T(8,128)(2,1)S(1)}, u32[]{:S(2)}, u32[]{:S(2)}) collective-permute-start(bf16[4,1,160,512]{3,2,0,1:T(8,128)(2,1)S(1)} %pad_maximum_fusion), channel_id=1, source_target_pairs={{0,1},{1,2},{2,3},{4,5},{5,6},{6,7},{8,9},{9,10},{10,11},{12,13},{... | collective-permute-start | bytes 1966088 | tf_op jit(solution)/shard_map/ppermute | solution.py:27
  90.7 1.5 collective-permute-done.4
  93.0 1.1 fusion.147
  94.1 1.1 fusion.146
  95.3 1.2 fusion.145
  96.4 1.1 fusion.144
  97.6 1.1 fusion.143
  98.7 1.2 fusion.142
  99.9 1.1 fusion.141
  101.0 1.1 fusion.140
  102.2 1.1 fusion.139
  103.3 1.2 fusion.138
  104.4 1.1 fusion.137
  105.6 1.2 fusion.136
  106.7 1.1 fusion.135
  107.9 1.2 fusion.134
  109.0 1.1 fusion.133
  110.2 1.1 fusion.132
  111.3 1.2 fusion.131
  112.5 1.2 fusion.130
  113.7 1.1 fusion.129
  114.9 1.1 fusion.128
  116.0 1.2 fusion.127
  117.1 1.1 fusion.126
  118.3 1.1 fusion.125
  119.4 1.1 fusion.124
  120.6 1.2 fusion.123
  121.7 1.2 fusion.122
  122.9 1.1 fusion.121
  124.1 238.6 %reduce-scatter.5.cloned.1.call-done = f32[3,3,3,64,256]{4,3,2,1,0:T(8,128)} async-done(((f32[3,3,3,512,256]{4,3,2,1,0:T(8,128)}), f32[3,3,3,64,256]{4,3,2,1,0:T(8,128)}) %reduce-scatter.5.cloned.1.call-update) | async-done | bytes 1769488 | tf_op jit(solution)/shard_map/reduce_scatter | solution.py:83
  362.7 5.9 %copy.18 = f32[3,3,3,64,256]{3,2,1,0,4:T(4,128)} copy(f32[3,3,3,64,256]{4,3,2,1,0:T(8,128)} %reduce-scatter.5.cloned.1.call-done) | data formatting | bytes 3538944
  368.7 5.8 %reshape.501 = f32[256,1728]{1,0:T(8,128)} reshape(f32[256,3,3,3,64]{4,3,2,1,0:T(4,128)} %bitcast.598) | data formatting | bytes 3538944
  374.5 39.4 %all-reduce.2 = (f32[1,512]{1,0:T(1,128)S(1)}, f32[1,512]{1,0:T(1,128)S(1)}) all-reduce(f32[1,512]{1,0:T(1,128)S(1)} %bitcast.628, f32[1,512]{1,0:T(1,128)S(1)} %bitcast.629), channel_id=1, replica_groups=mesh['tm'=8,'rows'=4] {'tm','rows'}, use_global_device_ids=true, to_apply=%region_12.13 | all-reduce | flops 1024 | bytes 8192 | tf_op jit(solution)/shard_map/psum | solution.py:133
  414.7 0.9 fusion.170
  415.6 1.6 reshape.502
  417.2 1.4 copy.19
  (114 shorter events, 17.7 us)
Async XLA Ops:
  7.2 355.6 %reduce-scatter.5.cloned.1.call-start = ((), (), s32[]{:S(2)}) async-start(), calls=%async_computation.2 | async-start | bytes 15925248 | tf_op jit(solution)/shard_map/reduce_scatter | solution.py:83
  7.2 46.2 %collective-permute-start = (bf16[2,1,160,256]{3,2,1,0:T(8,128)(2,1)}, bf16[2,1,160,256]{3,2,1,0:T(8,128)(2,1)S(1)}, u32[]{:S(2)}, u32[]{:S(2)}) collective-permute-start(bf16[2,1,160,256]{3,2,1,0:T(8,128)(2,1)} %param.13), channel_id=1, source_target_pairs={{4,0},{8,4},{12,8},{16,12},{20,16},{24,20},{28,24},{5,1},{9,5},{13... | collective-permute-start | bytes 491528 | tf_op jit(solution)/shard_map/ppermute | solution.py:16
  54.4 5.6 %collective-permute-start.2 = (bf16[4,1,160,256]{3,2,1,0:T(8,128)(2,1)S(1)}, bf16[4,1,160,256]{3,2,1,0:T(8,128)(2,1)S(1)}, u32[]{:S(2)}, u32[]{:S(2)}) collective-permute-start(bf16[4,1,160,256]{3,2,1,0:T(8,128)(2,1)S(1)} %pad_maximum_fusion.1), channel_id=1, source_target_pairs={{1,0},{2,1},{3,2},{5,4},{6,5},{7,6},{9,8},{10,9},{11,10},{13,12},{... | collective-permute-start | bytes 983048 | tf_op jit(solution)/shard_map/ppermute | solution.py:29
  55.7 4.3 %collective-permute-start.1 = (bf16[4,1,160,256]{3,2,1,0:T(8,128)(2,1)S(1)}, bf16[4,1,160,256]{3,2,1,0:T(8,128)(2,1)S(1)}, u32[]{:S(2)}, u32[]{:S(2)}) collective-permute-start(bf16[4,1,160,256]{3,2,1,0:T(8,128)(2,1)S(1)} %pad_maximum_fusion.1), channel_id=1, source_target_pairs={{0,1},{1,2},{2,3},{4,5},{5,6},{6,7},{8,9},{9,10},{10,11},{12,13},{... | collective-permute-start | bytes 983048 | tf_op jit(solution)/shard_map/ppermute | solution.py:27
  58.9 3.1 copy-start
  66.7 2.0 copy-start.1
  69.9 6.7 %copy-start.2 = (bf16[2,1,160,512]{3,2,1,0:T(8,128)(2,1)S(1)}, bf16[2,1,160,512]{3,2,1,0:T(8,128)(2,1)}, u32[]{:S(2)}) copy-start(bf16[2,1,160,512]{3,2,1,0:T(8,128)(2,1)} %param.9) | copy-start | bytes 983044
  69.9 6.7 %copy-start.3 = (f32[512]{0:T(512)S(1)}, f32[512]{0:T(512)}, u32[]{:S(2)}) copy-start(f32[512]{0:T(512)} %param.10) | copy-start | bytes 6148
  69.9 6.7 %copy-start.6 = (f32[512]{0:T(512)S(1)}, f32[512]{0:T(512)}, u32[]{:S(2)}) copy-start(f32[512]{0:T(512)} %param.11) | copy-start | bytes 6148
  77.0 5.9 %collective-permute-start.3 = (bf16[2,1,160,512]{3,2,0,1:T(8,128)(2,1)S(1)}, bf16[2,1,160,512]{3,2,0,1:T(8,128)(2,1)S(1)}, u32[]{:S(2)}, u32[]{:S(2)}) collective-permute-start(bf16[2,1,160,512]{3,2,0,1:T(8,128)(2,1)S(1)} %get-tuple-element.65), channel_id=1, source_target_pairs={{0,4},{4,8},{8,12},{12,16},{16,20},{20,24},{24,28},{1,5},{5,9},{9,... | collective-permute-start | bytes 983048 | tf_op jit(solution)/shard_map/ppermute | solution.py:16
  83.0 7.7 %collective-permute-start.5 = (bf16[4,1,160,512]{3,2,0,1:T(8,128)(2,1)S(1)}, bf16[4,1,160,512]{3,2,0,1:T(8,128)(2,1)S(1)}, u32[]{:S(2)}, u32[]{:S(2)}) collective-permute-start(bf16[4,1,160,512]{3,2,0,1:T(8,128)(2,1)S(1)} %pad_maximum_fusion), channel_id=1, source_target_pairs={{1,0},{2,1},{3,2},{5,4},{6,5},{7,6},{9,8},{10,9},{11,10},{13,12},{... | collective-permute-start | bytes 1966088 | tf_op jit(solution)/shard_map/ppermute | solution.py:29
  84.3 7.9 %collective-permute-start.4 = (bf16[4,1,160,512]{3,2,0,1:T(8,128)(2,1)S(1)}, bf16[4,1,160,512]{3,2,0,1:T(8,128)(2,1)S(1)}, u32[]{:S(2)}, u32[]{:S(2)}) collective-permute-start(bf16[4,1,160,512]{3,2,0,1:T(8,128)(2,1)S(1)} %pad_maximum_fusion), channel_id=1, source_target_pairs={{0,1},{1,2},{2,3},{4,5},{5,6},{6,7},{8,9},{9,10},{10,11},{12,13},{... | collective-permute-start | bytes 1966088 | tf_op jit(solution)/shard_map/ppermute | solution.py:27
  124.1 291.5 %reduce-scatter.7.cloned.1.call-start = ((), (), s32[]{:S(2)}) async-start(), calls=%async_computation.3 | async-start | bytes 2293760
  413.9 4.7 %copy-start.4 = (f32[1,512]{1,0:T(1,128)}, f32[1,512]{1,0:T(1,128)S(1)}, u32[]{:S(2)}) copy-start(f32[1,512]{1,0:T(1,128)S(1)} %get-tuple-element.42) | copy-start | bytes 6148
  413.9 4.7 %copy-start.5 = (f32[1,512]{1,0:T(1,128)}, f32[1,512]{1,0:T(1,128)S(1)}, u32[]{:S(2)}) copy-start(f32[1,512]{1,0:T(1,128)S(1)} %get-tuple-element.43) | copy-start | bytes 6148
Sparse Core Ops, SparseCore 0:
  124.2 238.5 reduce-scatter.4
  374.6 29.0 reduce-scatter.6
where the time goes:
time: 426 us; the launch traced here: 425 us
  waiting for transfers between devices  245 us (58%)
  blocking collectives  82.6 us (19%)
  matrix products  45 us (11%)
  local copies, waits for them, and re-layouts  16.4 us (4%)
  starting transfers between devices  14.7 us (3%)
  between operations  14.6 us (3%)
  other arithmetic  7.35 us (2%)
    reduce_scatter x1, waiting for transfers between devices, on_device(): lax.psum_scatter(local_grad, 'tm', scatter_dimension=3, tiled=True)  239 us
    psum x1, blocking collectives, on_device(): lax.psum((selector[:, None] * local_sum, selector[:, None] * local_sq), (...  43.2 us
    psum x1, blocking collectives, on_device(): lax.psum((selector[:, None] * local_gain, selector[:, None] * local_bias)...  39.4 us
    dot_general x27, matrix products, on_device(): lax.dot_general(slab, up_flat, (((0,), (0,)), ((), ())), preferred_elemen...  31 us
    unnamed x19, local copies, waits for them, and re-layouts  15 us
    ppermute x2, starting transfers between devices, padded(): lax.ppermute(tail, axis, [(i, (i + 1) % count) for i in range(ends)])  9.46 us
  transfers between devices with their start and end apart: 8, of which 3 were waited for; matrix products, arithmetic and copies ran while one was open for 1% of the time, Pallas kernels for 0%

commit v1 on v0

--- a/solution.py
+++ b/solution.py
@@ -1,6 +1,10 @@
+import functools
+
 import jax
 import jax.numpy as jnp
 from jax import lax
+from jax.experimental import pallas as pl
+from jax.experimental.pallas import tpu as pltpu
 from jax.sharding import PartitionSpec as P
 
 GROUPS = 32
@@ -150,9 +154,448 @@
     return (grad_features, grad_weight, grad_gain, grad_bias)
 
 
+MESH = pl.DeviceIdType.MESH
+F32 = jnp.float32
+BF16 = jnp.bfloat16
+
+
+def group_total(value, group_size):
+    lanes = value.shape[1]
+    lane = lax.broadcasted_iota(jnp.int32, value.shape, 1)
+    step = 1
+    while step < group_size:
+        up = pltpu.roll(value, step, 1)
+        down = pltpu.roll(value, lanes - step, 1)
+        value = value + jnp.where((lane & step) != 0, up, down)
+        step *= 2
+    return value
+
+
+def pack_pair(first, second):
+    lane = lax.broadcasted_iota(jnp.int32, first.shape, 1)
+    low = lane < 64
+    even = jnp.where(low, first, pltpu.roll(second, 64, 1))
+    odd = jnp.where(low, pltpu.roll(first, 64, 1), second)
+    return even.astype(BF16), odd.astype(BF16)
+
+
+def kernel(
+    dims,
+    feat, gain_ref, bias_ref, weight_hbm, up_ref,
+    gf_ref, gw_ref, gg_ref, gb_ref,
+    weight, ext, acc, normed_s, dact_s, hpack, hall, upack, uall, ut, gacc,
+    st_r, st_t, sg_r, sg_t,
+    w_sem,
+    st_rs, st_rr, st_ts, st_tr, sg_rs, sg_rr, sg_ts, sg_tr,
+    ha_s, ha_r, u1_s, u1_r, u2_s, u2_r, h1_s, h1_r, h2_s, h2_r,
+):
+    nt, nr, cols, chans, outs, group_size = dims
+    pos = 2 * cols
+    a = lax.axis_index("tm")
+    b = lax.axis_index("rows")
+    count = float(nt * nr * pos * group_size)
+
+    w_copy = pltpu.make_async_copy(weight_hbm, weight, w_sem)
+    w_copy.start()
+
+    barrier = pltpu.get_barrier_semaphore()
+    tm_peers = [lax.rem(a + d, nt) for d in range(1, nt)]
+    row_peers = [lax.rem(b + d, nr) for d in range(1, nr)]
+    for peer in row_peers:
+        pl.semaphore_signal(barrier, inc=1, device_id=(a, peer), device_id_type=MESH)
+    for peer in tm_peers:
+        pl.semaphore_signal(barrier, inc=1, device_id=(peer, b), device_id_type=MESH)
+
+    def to_row(src, dst, ssem, rsem, peer):
+        return pltpu.make_async_remote_copy(
+            src_ref=src, dst_ref=dst, send_sem=ssem, recv_sem=rsem,
+            device_id=(a, peer), device_id_type=MESH,
+        )
+
+    def to_tm(src, dst, ssem, rsem, peer):
+        return pltpu.make_async_remote_copy(
+            src_ref=src, dst_ref=dst, send_sem=ssem, recv_sem=rsem,
+            device_id=(peer, b), device_id_type=MESH,
+        )
+
+    xs = feat[...].astype(F32)
+    st_r[b, 0:1] = jnp.sum(xs, axis=0, keepdims=True)
+    st_r[b, 1:2] = jnp.sum(xs * xs, axis=0, keepdims=True)
+    st_r[b, 2:8] = jnp.zeros((6, chans), F32)
+
+    for q in range(outs // 128):
+        lanes = slice(q * 128, q * 128 + 128)
+        even, odd = pack_pair(
+            up_ref[0:cols, lanes].astype(F32), up_ref[cols:pos, lanes].astype(F32)
+        )
+        upack[2 * q] = even
+        upack[2 * q + 1] = odd
+    ext[1, 0:pos] = up_ref[...]
+    zeros_ext = jnp.zeros((pos, outs), BF16)
+
+    @pl.when(b == 0)
+    def _():
+        ext[0, 0:pos] = zeros_ext
+
+    @pl.when(b == nr - 1)
+    def _():
+        ext[2, 0:pos] = zeros_ext
+
+    @pl.when(a == nt - 1)
+    def _():
+        for r in range(3):
+            ext[r, pos : 2 * pos] = zeros_ext
+
+    pl.semaphore_wait(barrier, nt + nr - 2)
+
+    for peer in row_peers:
+        to_row(st_r.at[b], st_r.at[b], st_rs.at[peer], st_rr.at[b], peer).start()
+
+    def u1_copy(src_row, peer):
+        return to_row(
+            upack.at[peer], uall.at[src_row, pl.ds(a * cols, cols)],
+            u1_s.at[peer], u1_r.at[src_row], peer,
+        )
+
+    for peer in row_peers:
+        u1_copy(b, peer).start()
+    own = pl.ds(pl.multiple_of(a * cols, 32), cols)
+    uall[b, own] = upack[b]
+
+    def to_above():
+        return to_row(up_ref, ext.at[2, pl.ds(0, pos)], ha_s.at[0], ha_r.at[0], lax.rem(b + nr - 1, nr))
+
+    def to_below():
+        return to_row(up_ref, ext.at[0, pl.ds(0, pos)], ha_s.at[1], ha_r.at[1], lax.rem(b + 1, nr))
+
+    @pl.when(b > 0)
+    def _():
+        to_above().start()
+
+    @pl.when(b < nr - 1)
+    def _():
+        to_below().start()
+
+    for peer in row_peers:
+        to_row(st_r.at[b], st_r.at[peer], st_rs.at[peer], st_rr.at[peer], peer).wait_recv()
+    part = st_r[0]
+    for r in range(1, nr):
+        part = part + st_r[r]
+    st_t[a] = part
+    for peer in tm_peers:
+        to_tm(st_t.at[a], st_t.at[a], st_ts.at[peer], st_tr.at[a], peer).start()
+
+    for peer in row_peers:
+        u1_copy(peer, peer).wait_recv()
+
+    def u2_copy(src, peer):
+        place = pl.ds(src * cols, cols)
+        return to_tm(
+            uall.at[:, place], uall.at[:, place], u2_s.at[peer], u2_r.at[src], peer
+        )
+
+    for peer in tm_peers:
+        to_tm(st_t.at[a], st_t.at[peer], st_ts.at[peer], st_tr.at[peer], peer).wait_recv()
+    for peer in tm_peers:
+        u2_copy(a, peer).start()
+    total = st_t[0]
+    for t in range(1, nt):
+        total = total + st_t[t]
+    total = group_total(total, group_size) / count
+    centre = total[0:1]
+    inverse = lax.rsqrt(total[1:2] - centre * centre + epsilon)
+    gain = gain_ref[...]
+    bias = bias_ref[...]
+    for q in range(chans // 128):
+        lanes = slice(q * 128, q * 128 + 128)
+        halves = []
+        for f in range(2):
+            rows = slice(f * cols, f * cols + cols)
+            normed = (feat[rows, lanes].astype(F32) - centre[:, lanes]) * inverse[:, lanes]
+            preact = normed * gain[:, lanes] + bias[:, lanes]
+            sig = jax.nn.sigmoid(preact)
+            normed_s[rows, lanes] = normed
+            dact_s[rows, lanes] = sig * (1.0 + preact * (1.0 - sig))
+            halves.append(preact * sig)
+        even, odd = pack_pair(*halves)
+        hpack[2 * q] = even
+        hpack[2 * q + 1] = odd
+
+    def h1_copy(src, peer):
+        return to_tm(
+            hpack.at[peer], hall.at[b, pl.ds((src + 1) * cols, cols)],
+            h1_s.at[peer], h1_r.at[src], peer,
+        )
+
+    for peer in tm_peers:
+        h1_copy(a, peer).start()
+    hall[b, pl.ds(pl.multiple_of((a + 1) * cols, 32), cols)] = hpack[a]
+
+    @pl.when(b > 0)
+    def _():
+        to_below().wait_recv()
+
+    @pl.when(b < nr - 1)
+    def _():
+        to_above().wait_recv()
+
+    def to_earlier():
+        return to_tm(
+            ext.at[:, pl.ds(0, pos)], ext.at[:, pl.ds(pos, pos)], ha_s.at[2], ha_r.at[2], lax.rem(a + nt - 1, nt)
+        )
+
+    @pl.when(a > 0)
+    def _():
+        to_earlier().start()
+
+    w_copy.wait()
+
+    def dot_t(lhs, rhs):
+        return lax.dot_general(lhs, rhs, (((1,), (1,)), ((), ())), preferred_element_type=F32)
+
+    def dense_own(c, carry):
+        val = dot_t(ext[2, 0:pos], weight[2, 0, c])
+        for tap in range(1, 3):
+            val = val + dot_t(ext[2 - tap, 0:pos], weight[2, tap, c])
+        acc[c] = val
+        return carry
+
+    lax.fori_loop(0, 3, dense_own, 0)
+
+    for peer in tm_peers:
+        h1_copy(peer, peer).wait_recv()
+
+    def h2_copy(src, peer):
+        place = pl.ds(cols, nt * cols)
+        return to_row(
+            hall.at[src, place], hall.at[src, place], h2_s.at[peer], h2_r.at[src], peer
+        )
+
+    for peer in row_peers:
+        h2_copy(b, peer).start()
+
+    @pl.when(a < nt - 1)
+    def _():
+        to_earlier().wait_recv()
+
+    def dense_rest(c, carry):
+        val = acc[c]
+        for tap in range(3):
+            val = val + dot_t(ext[2 - tap, cols : cols + pos], weight[1, tap, c])
+            val = val + dot_t(ext[2 - tap, pos : 2 * pos], weight[0, tap, c])
+        acc[c] = val
+        return carry
+
+    lax.fori_loop(0, 3, dense_rest, 0)
+
+    @pl.when(a == 0)
+    def _():
+        def dense_first(c, carry):
+            val = acc[c, 0:cols]
+            for tap in range(3):
+                val = val + dot_t(ext[2 - tap, 0:cols], weight[0, tap, c])
+                val = val + dot_t(ext[2 - tap, 0:cols], weight[1, tap, c])
+                val = val + dot_t(ext[2 - tap, cols:pos], weight[0, tap, c])
+            acc[c, 0:cols] = val
+            return carry
+
+        lax.fori_loop(0, 3, dense_first, 0)
+
+    sg_r[b, 2:8] = jnp.zeros((6, chans), F32)
+    for q in range(chans // 128):
+        lanes = slice(q * 128, q * 128 + 128)
+        sum_gain = jnp.zeros((1, 128), F32)
+        sum_bias = jnp.zeros((1, 128), F32)
+        for f in range(2):
+            rows = slice(f * cols, f * cols + cols)
+            place = lax.broadcasted_iota(jnp.int32, (cols, 128), 0)
+            right = jnp.where(
+                place == cols - 1, 0.0, pltpu.roll(acc[0, rows, lanes], cols - 1, 0)
+            )
+            left = jnp.where(place == 0, 0.0, pltpu.roll(acc[2, rows, lanes], 1, 0))
+            act = (acc[1, rows, lanes] + right + left) * dact_s[rows, lanes]
+            dact_s[rows, lanes] = act
+            sum_gain = sum_gain + jnp.sum(act * normed_s[rows, lanes], axis=0, keepdims=True)
+            sum_bias = sum_bias + jnp.sum(act, axis=0, keepdims=True)
+        sg_r[b, 0:1, lanes] = sum_gain
+        sg_r[b, 1:2, lanes] = sum_bias
+    for peer in row_peers:
+        to_row(sg_r.at[b], sg_r.at[b], sg_rs.at[peer], sg_rr.at[b], peer).start()
+
+    for peer in tm_peers:
+        u2_copy(peer, peer).wait_recv()
+    half = nt * cols // 2
+    for part_index in range(2):
+        rows = slice(part_index * half, part_index * half + half)
+        place = lax.broadcasted_iota(jnp.int32, (half, 128), 0) % cols
+
+        def turn(i, carry, rows=rows, place=place):
+            block = uall[i, rows].astype(F32)
+            ahead = jnp.where(place == cols - 1, 0.0, pltpu.roll(block, half - 1, 0))
+            behind = jnp.where(place == 0, 0.0, pltpu.roll(block, 1, 0))
+            ut[i, 0:128, rows] = ahead.T.astype(BF16)
+            ut[i, 128:256, rows] = block.T.astype(BF16)
+            ut[i, 256:384, rows] = behind.T.astype(BF16)
+            return carry
+
+        lax.fori_loop(0, nr, turn, 0)
+
+    for peer in row_peers:
+        to_row(sg_r.at[b], sg_r.at[peer], sg_rs.at[peer], sg_rr.at[peer], peer).wait_recv()
+    part = sg_r[0]
+    for r in range(1, nr):
+        part = part + sg_r[r]
+    sg_t[a] = part
+    for peer in tm_peers:
+        to_tm(sg_t.at[a], sg_t.at[a], sg_ts.at[peer], sg_tr.at[a], peer).start()
+
+    for peer in row_peers:
+        h2_copy(peer, peer).wait_recv()
+    low = lax.broadcasted_iota(jnp.int32, (cols, 128), 1) < 64
+    for r in range(nr):
+        block = hall[r, cols : 2 * cols].astype(F32)
+        hall[r, 0:cols] = jnp.where(low, block, pltpu.roll(block, 64, 1)).astype(BF16)
+    span = nt * cols
+    for r in range(nr):
+        both = jnp.concatenate([hall[r, 0:span], hall[r, cols : cols + span]], axis=1)
+        for tap in range(3):
+            i = r - tap + 1
+            if 0 <= i < nr:
+                prod = jnp.dot(ut[i], both, preferred_element_type=F32)
+                first = r == max(0, tap - 1)
+                gacc[tap] = prod if first else gacc[tap] + prod
+    for tap in range(3):
+        for c in range(3):
+            base = c * 128
+            even = gacc[tap, base : base + 64]
+            odd = gacc[tap, base + 64 : base + 128]
+            turned = (even + pltpu.roll(odd, 192, 1)).T
+            for t in range(3):
+                gw_ref[t * 9 + tap * 3 + c] = turned[t * 64 : t * 64 + 64]
+
+    for peer in tm_peers:
+        to_tm(sg_t.at[a], sg_t.at[peer], sg_ts.at[peer], sg_tr.at[peer], peer).wait_recv()
+    total = sg_t[0]
+    for t in range(1, nt):
+        total = total + sg_t[t]
+    gg_ref[...] = total[0:1]
+    gb_ref[...] = total[1:2]
+    terms = group_total(total * gain, group_size) / count
+    second_term = terms[0:1]
+    first_term = terms[1:2]
+    for q in range(chans // 128):
+        lanes = slice(q * 128, q * 128 + 128)
+        gf_ref[:, lanes] = (
+            inverse[:, lanes]
+            * (
+                dact_s[:, lanes] * gain[:, lanes]
+                - first_term[:, lanes]
+                - normed_s[:, lanes] * second_term[:, lanes]
+            )
+        ).astype(BF16)
+
+    for peer in row_peers:
+        to_row(st_r.at[b], st_r.at[b], st_rs.at[peer], st_rr.at[b], peer).wait_send()
+        to_row(sg_r.at[b], sg_r.at[b], sg_rs.at[peer], sg_rr.at[b], peer).wait_send()
+        u1_copy(b, peer).wait_send()
+        h2_copy(b, peer).wait_send()
+    for peer in tm_peers:
+        to_tm(st_t.at[a], st_t.at[a], st_ts.at[peer], st_tr.at[a], peer).wait_send()
+        to_tm(sg_t.at[a], sg_t.at[a], sg_ts.at[peer], sg_tr.at[a], peer).wait_send()
+        u2_copy(a, peer).wait_send()
+        h1_copy(a, peer).wait_send()
+
+    @pl.when(b > 0)
+    def _():
+        to_above().wait_send()
+
+    @pl.when(b < nr - 1)
+    def _():
+        to_below().wait_send()
+
+    @pl.when(a > 0)
+    def _():
+        to_earlier().wait_send()
+
+
+def fused(features, norm_gain, norm_bias, weight, upstream):
+    frames_dev, rows_dev, cols, chans = features.shape
+    outs = upstream.shape[3]
+    nt, nr = lax.axis_size("tm"), lax.axis_size("rows")
+    pos = frames_dev * rows_dev * cols
+    dims = (nt, nr, cols, chans, outs, chans // GROUPS)
+    vmem = pl.BlockSpec(memory_space=pltpu.VMEM)
+    dma = pltpu.SemaphoreType.DMA
+    span = nt * cols
+    gf, gw, gg, gb = pl.pallas_call(
+        functools.partial(kernel, dims),
+        out_shape=(
+            jax.ShapeDtypeStruct((pos, chans), BF16),
+            jax.ShapeDtypeStruct((27, 64, 64), F32),
+            jax.ShapeDtypeStruct((1, chans), F32),
+            jax.ShapeDtypeStruct((1, chans), F32),
+        ),
+        in_specs=[vmem, vmem, vmem, pl.BlockSpec(memory_space=pl.ANY), vmem],
+        out_specs=(vmem, vmem, vmem, vmem),
+        scratch_shapes=[
+            pltpu.VMEM((3, 3, 3, chans, outs), BF16),
+            pltpu.VMEM((3, 2 * pos, outs), BF16),
+            pltpu.VMEM((3, pos, chans), F32),
+            pltpu.VMEM((pos, chans), F32),
+            pltpu.VMEM((pos, chans), F32),
+            pltpu.VMEM((nt, cols, 128), BF16),
+            pltpu.VMEM((nr, span + cols, 128), BF16),
+            pltpu.VMEM((nr, cols, 128), BF16),
+            pltpu.VMEM((nr, span, 128), BF16),
+            pltpu.VMEM((nr, 384, span), BF16),
+            pltpu.VMEM((3, 384, 256), F32),
+            pltpu.VMEM((nr, 8, chans), F32),
+            pltpu.VMEM((nt, 8, chans), F32),
+            pltpu.VMEM((nr, 8, chans), F32),
+            pltpu.VMEM((nt, 8, chans), F32),
+            dma,
+            dma((nr,)), dma((nr,)), dma((nt,)), dma((nt,)),
+            dma((nr,)), dma((nr,)), dma((nt,)), dma((nt,)),
+            dma((3,)), dma((3,)),
+            dma((nr,)), dma((nr,)), dma((nt,)), dma((nt,)),
+            dma((nt,)), dma((nt,)), dma((nr,)), dma((nr,)),
+        ],
+        compiler_params=pltpu.CompilerParams(
+            collective_id=0, has_side_effects=True, vmem_limit_bytes=48 * 1024 * 1024
+        ),
+    )(
+        features.reshape(pos, chans),
+        norm_gain.reshape(1, chans),
+        norm_bias.reshape(1, chans),
+        weight,
+        upstream.reshape(pos, outs),
+    )
+    return (
+        gf.reshape(features.shape),
+        gw.reshape(3, 3, 3, 64, 64),
+        gg.reshape(chans),
+        gb.reshape(chans),
+    )
+
+
+def body(features, norm_gain, norm_bias, weight, upstream):
+    frames_dev, rows_dev, cols, chans = features.shape
+    outs = upstream.shape[3]
+    nt, nr = lax.axis_size("tm"), lax.axis_size("rows")
+    fits = (
+        CLIPS == 1
+        and (frames_dev, rows_dev) == (2, 1)
+        and (chans, outs) == (64 * nt, 64 * nr)
+        and cols % 32 == 0
+        and (nt * cols) % 256 == 0
+    )
+    run = fused if fits else on_device
+    return run(features, norm_gain, norm_bias, weight, upstream)
+
+
 def solution(mesh):
     in_specs = (P("tm", "rows", None, None), P(), P(), P(), P("tm", "rows", None, None))
     out_specs = (P("tm", "rows", None, None), P(None, None, None, "tm", "rows"), P(), P())
     return jax.shard_map(
-        on_device, mesh=mesh, in_specs=in_specs, out_specs=out_specs, check_vma=False
-    )
+        body, mesh=mesh, in_specs=in_specs, out_specs=out_specs, check_vma=False
+    )

time: 426 us -> 79.6 us (0.19)
  waiting for transfers between devices: 245 us -> 0 us
  blocking collectives: 82.6 us -> 0 us
  Pallas kernels: 0 us -> 72.7 us
  matrix products: 45 us -> 0 us
  starting transfers between devices: 14.7 us -> 0 us
  between operations: 14.6 us -> 0.65 us
  local copies, waits for them, and re-layouts: 16.4 us -> 6.04 us
  other arithmetic: 7.35 us -> 0 us
    reduce_scatter x1 -> x0, waiting for transfers between devices: 239 us -> none  [on_device(): lax.psum_scatter(local_grad, 'tm', scatter_dimension=3, tiled=True)]
    psum x2 -> x0, blocking collectives: 82.6 us -> none  [the longest x1 43.2 us: on_device(): lax.psum((selector[:, None] * local_sum, selector[:, None] * local_sq), (...]
    pallas_call x0 -> x1, Pallas kernels: none -> 72.7 us  [fused(): pl.pallas_call(functools.partial(kernel, dims), out_shape=(jax.ShapeDtype...]
    dot_general x81 -> x0, matrix products: 45 us -> none  [the longest x27 31 us: on_device(): lax.dot_general(slab, up_flat, (((0,), (0,)), ((), ())), preferred_elemen...]
    ppermute x6 -> x0, starting transfers between devices: 14.6 us -> none  [the longest x2 9.46 us: padded(): lax.ppermute(tail, axis, [(i, (i + 1) % count) for i in range(ends)])]
    unnamed x19 -> x12, local copies, waits for them, and re-layouts: 15 us -> 6.04 us
    ppermute x6 -> x0, waiting for transfers between devices: 6.02 us -> none  [the longest x2 4.54 us: from_behind(): lax.ppermute(value, axis, [(source, source + steps) for source in range(i...]
    concatenate x5 -> x0, other arithmetic: 4.3 us -> none  [the longest x2 2.23 us: padded(): jnp.concatenate([lax.ppermute(tail, axis, [(i, (i + 1) % count) for i in...]
  transfers between devices with their start and end apart: 8 -> 0, of which waited for: 3 -> 0; matrix products, arithmetic and copies ran while one was open for 1% -> 0% of each run, Pallas kernels for 0% -> 0%
where the time goes in v1:
time: 79.6 us; the launch traced here: 79.4 us
  Pallas kernels  72.7 us (91%)
  local copies, waits for them, and re-layouts  6.04 us (8%)
    pallas_call x1, Pallas kernels, fused(): pl.pallas_call(functools.partial(kernel, dims), out_shape=(jax.ShapeDtype...  72.7 us
    unnamed x12, local copies, waits for them, and re-layouts  6.04 us

profile of v1, /device:TPU:0, one launch (start us, length us, event | category | flops | bytes accessed | tf_op | source)
XLA Modules:
  0.0 79.4 jit_solution(10437623287228664073)
XLA Ops:
  0.6 0.0 copy-start
  0.6 1.0 %copy-done = bf16[2,1,160,512]{3,2,1,0:T(8,128)(2,1)S(1)} copy-done((bf16[2,1,160,512]{3,2,1,0:T(8,128)(2,1)S(1)}, bf16[2,1,160,512]{3,2,1,0:T(8,128)(2,1)}, u32[]{:S(2)}) %copy-start) | copy-done | bytes 327704
  1.6 0.0 copy-start.1
  1.6 0.9 %copy-done.1 = bf16[2,1,160,256]{3,2,1,0:T(8,128)(2,1)S(1)} copy-done((bf16[2,1,160,256]{3,2,1,0:T(8,128)(2,1)S(1)}, bf16[2,1,160,256]{3,2,1,0:T(8,128)(2,1)}, u32[]{:S(2)}) %copy-start.1) | copy-done | bytes 163864
  2.5 0.0 copy-start.2
  2.5 0.7 copy-done.2
  3.2 0.0 copy-start.3
  3.2 0.7 copy-done.3
  3.9 72.7 %shard_map.84 = (bf16[320,512]{1,0:T(8,128)(2,1)S(1)}, f32[27,64,64]{2,1,0:T(8,128)S(1)}, f32[1,512]{1,0:T(1,128)S(1)}, f32[1,512]{1,0:T(1,128)S(1)}) custom-call(bf16[320,512]{1,0:T(8,128)(2,1)S(1)} %bitcast.11, f32[1,512]{1,0:T(1,128)S(1)} %bitcast.14, f32[1,512]{1,0:T(1,128)S(1)} %bitcast.15, bf16[3,3,3,512,256]{4,3,2,1,0:T(8,128)(2,1)} %weight_hbm.1, ...), custom_call_target="tpu_custom_call" | custom-call | tf_op jit(solution)/shard_map/pallas_call | solution.py:530
  76.6 0.7 copy.14
  77.3 0.9 %copy.15 = f32[3,3,3,64,64]{4,3,2,1,0:T(8,128)} copy(f32[3,3,3,64,64]{4,3,2,1,0:T(8,128)S(1)} %bitcast.10) | data formatting | bytes 884736
  78.2 0.6 copy.16
  78.8 0.6 copy.17
Async XLA Ops:
  0.6 1.0 %copy-start = (bf16[2,1,160,512]{3,2,1,0:T(8,128)(2,1)S(1)}, bf16[2,1,160,512]{3,2,1,0:T(8,128)(2,1)}, u32[]{:S(2)}) copy-start(bf16[2,1,160,512]{3,2,1,0:T(8,128)(2,1)} %param.5) | copy-start | bytes 983044
  1.6 0.9 %copy-start.1 = (bf16[2,1,160,256]{3,2,1,0:T(8,128)(2,1)S(1)}, bf16[2,1,160,256]{3,2,1,0:T(8,128)(2,1)}, u32[]{:S(2)}) copy-start(bf16[2,1,160,256]{3,2,1,0:T(8,128)(2,1)} %param.9) | copy-start | bytes 491524
  2.5 0.7 copy-start.2
  3.2 0.7 copy-start.3

commit v2 on v1

--- a/solution.py
+++ b/solution.py
@@ -181,13 +181,13 @@
 
 def kernel(
     dims,
-    feat, gain_ref, bias_ref, weight_hbm, up_ref,
+    feat_hbm, gain_hbm, bias_hbm, weight_hbm, up_hbm,
     gf_ref, gw_ref, gg_ref, gb_ref,
-    weight, ext, acc, normed_s, dact_s, hpack, hall, upack, uall, ut, gacc,
+    feat, gain_ref, bias_ref, up_ref, weight, ext, acc, normed_s, dact_s, hpack, hall, upack, uall, ut, gacc,
     st_r, st_t, sg_r, sg_t,
-    w_sem,
+    in_sem,
     st_rs, st_rr, st_ts, st_tr, sg_rs, sg_rr, sg_ts, sg_tr,
-    ha_s, ha_r, u1_s, u1_r, u2_s, u2_r, h1_s, h1_r, h2_s, h2_r,
+    ha_s, ha_r, u1_s, u1_r, u2_s, u2_r, u3_s, h1_s, h1_r, hc_s, hc_r, hy_s, hy_r, hf_s, hf_r,
 ):
     nt, nr, cols, chans, outs, group_size = dims
     pos = 2 * cols
@@ -195,12 +195,25 @@
     b = lax.axis_index("rows")
     count = float(nt * nr * pos * group_size)
 
-    w_copy = pltpu.make_async_copy(weight_hbm, weight, w_sem)
-    w_copy.start()
+    nq = chans // 128
+    f_copy = pltpu.make_async_copy(feat_hbm, feat, in_sem.at[0])
+    c_copy = pltpu.make_async_copy(up_hbm, up_ref, in_sem.at[1])
+    g_copy = pltpu.make_async_copy(gain_hbm, gain_ref, in_sem.at[2])
+    b_copy = pltpu.make_async_copy(bias_hbm, bias_ref, in_sem.at[3])
+    w_copy = pltpu.make_async_copy(weight_hbm, weight, in_sem.at[4])
+    f_copy.start()
+    c_copy.start()
+    g_copy.start()
+    b_copy.start()
 
     barrier = pltpu.get_barrier_semaphore()
     tm_peers = [lax.rem(a + d, nt) for d in range(1, nt)]
     row_peers = [lax.rem(b + d, nr) for d in range(1, nr)]
+    line_peers = [lax.rem(a + d, nt) for d in range(2, nt, 2)]
+    side = a + 1 - 2 * lax.rem(a, 2)
+    twin = b + 1 - 2 * lax.rem(b, 2)
+    across = lax.rem(b + 2, nr)
+    far = lax.rem(twin + 2, nr)
     for peer in row_peers:
         pl.semaphore_signal(barrier, inc=1, device_id=(a, peer), device_id_type=MESH)
     for peer in tm_peers:
@@ -218,11 +231,17 @@
             device_id=(peer, b), device_id_type=MESH,
         )
 
-    xs = feat[...].astype(F32)
-    st_r[b, 0:1] = jnp.sum(xs, axis=0, keepdims=True)
-    st_r[b, 1:2] = jnp.sum(xs * xs, axis=0, keepdims=True)
-    st_r[b, 2:8] = jnp.zeros((6, chans), F32)
-
+    f_copy.wait()
+    w_copy.start()
+    for q in range(nq):
+        xs = feat[:, q * 128 : q * 128 + 128].astype(F32)
+        st_r[b, q : q + 1] = jnp.sum(xs, axis=0, keepdims=True)
+        st_r[b, nq + q : nq + q + 1] = jnp.sum(xs * xs, axis=0, keepdims=True)
+    pl.semaphore_wait(barrier, nt + nr - 2)
+    for peer in row_peers:
+        to_row(st_r.at[b], st_r.at[b], st_rs.at[peer], st_rr.at[b], peer).start()
+
+    c_copy.wait()
     for q in range(outs // 128):
         lanes = slice(q * 128, q * 128 + 128)
         even, odd = pack_pair(
@@ -230,27 +249,6 @@
         )
         upack[2 * q] = even
         upack[2 * q + 1] = odd
-    ext[1, 0:pos] = up_ref[...]
-    zeros_ext = jnp.zeros((pos, outs), BF16)
-
-    @pl.when(b == 0)
-    def _():
-        ext[0, 0:pos] = zeros_ext
-
-    @pl.when(b == nr - 1)
-    def _():
-        ext[2, 0:pos] = zeros_ext
-
-    @pl.when(a == nt - 1)
-    def _():
-        for r in range(3):
-            ext[r, pos : 2 * pos] = zeros_ext
-
-    pl.semaphore_wait(barrier, nt + nr - 2)
-
-    for peer in row_peers:
-        to_row(st_r.at[b], st_r.at[b], st_rs.at[peer], st_rr.at[b], peer).start()
-
     def u1_copy(src_row, peer):
         return to_row(
             upack.at[peer], uall.at[src_row, pl.ds(a * cols, cols)],
@@ -262,19 +260,60 @@
     own = pl.ds(pl.multiple_of(a * cols, 32), cols)
     uall[b, own] = upack[b]
 
+    here, ahead_rows = pl.ds(0, pos), pl.ds(pos, pos)
+    above, below = lax.rem(b + nr - 1, nr), lax.rem(b + 1, nr)
+
     def to_above():
-        return to_row(up_ref, ext.at[2, pl.ds(0, pos)], ha_s.at[0], ha_r.at[0], lax.rem(b + nr - 1, nr))
+        return to_row(up_ref, ext.at[2, here], ha_s.at[0], ha_r.at[0], above)
 
     def to_below():
-        return to_row(up_ref, ext.at[0, pl.ds(0, pos)], ha_s.at[1], ha_r.at[1], lax.rem(b + 1, nr))
-
-    @pl.when(b > 0)
+        return to_row(up_ref, ext.at[0, here], ha_s.at[1], ha_r.at[1], below)
+
+    def to_earlier():
+        return to_tm(
+            up_ref, ext.at[1, ahead_rows], ha_s.at[2], ha_r.at[2], lax.rem(a + nt - 1, nt)
+        )
+
+    def next_above():
+        return to_row(
+            ext.at[1, ahead_rows], ext.at[2, ahead_rows], ha_s.at[3], ha_r.at[3], above
+        )
+
+    def next_below():
+        return to_row(
+            ext.at[1, ahead_rows], ext.at[0, ahead_rows], ha_s.at[4], ha_r.at[4], below
+        )
+
+    not_top, not_bottom = b > 0, b < nr - 1
+    not_first, not_last = a > 0, a < nt - 1
+
+    @pl.when(not_first)
+    def _():
+        to_earlier().start()
+
+    @pl.when(not_top)
     def _():
         to_above().start()
 
-    @pl.when(b < nr - 1)
+    @pl.when(not_bottom)
     def _():
         to_below().start()
+
+    ext[1, 0:pos] = up_ref[...]
+    zeros_ext = jnp.zeros((2 * pos, outs), BF16)
+
+    @pl.when(b == 0)
+    def _():
+        ext[0] = zeros_ext
+
+    @pl.when(b == nr - 1)
+    def _():
+        ext[2] = zeros_ext
+
+    @pl.when(a == nt - 1)
+    def _():
+        for r in range(3):
+            ext[r, pos : 2 * pos] = zeros_ext[0:pos]
 
     for peer in row_peers:
         to_row(st_r.at[b], st_r.at[peer], st_rs.at[peer], st_rr.at[peer], peer).wait_recv()
@@ -294,25 +333,33 @@
             uall.at[:, place], uall.at[:, place], u2_s.at[peer], u2_r.at[src], peer
         )
 
+    def u3_copy(src):
+        place = pl.ds(src * cols, cols)
+        return to_tm(
+            uall.at[:, place], uall.at[:, place], u3_s.at[src], u2_r.at[src], side
+        )
+
+    for peer in line_peers:
+        u2_copy(a, peer).start()
+    u3_copy(a).start()
+
     for peer in tm_peers:
         to_tm(st_t.at[a], st_t.at[peer], st_ts.at[peer], st_tr.at[peer], peer).wait_recv()
-    for peer in tm_peers:
-        u2_copy(a, peer).start()
     total = st_t[0]
     for t in range(1, nt):
         total = total + st_t[t]
     total = group_total(total, group_size) / count
-    centre = total[0:1]
-    inverse = lax.rsqrt(total[1:2] - centre * centre + epsilon)
-    gain = gain_ref[...]
-    bias = bias_ref[...]
-    for q in range(chans // 128):
+    centre = total[0:nq]
+    inverse = lax.rsqrt(total[nq : 2 * nq] - centre * centre + epsilon)
+    g_copy.wait()
+    b_copy.wait()
+    for q in range(nq):
         lanes = slice(q * 128, q * 128 + 128)
         halves = []
         for f in range(2):
             rows = slice(f * cols, f * cols + cols)
-            normed = (feat[rows, lanes].astype(F32) - centre[:, lanes]) * inverse[:, lanes]
-            preact = normed * gain[:, lanes] + bias[:, lanes]
+            normed = (feat[rows, lanes].astype(F32) - centre[q : q + 1]) * inverse[q : q + 1]
+            preact = normed * gain_ref[:, lanes] + bias_ref[:, lanes]
             sig = jax.nn.sigmoid(preact)
             normed_s[rows, lanes] = normed
             dact_s[rows, lanes] = sig * (1.0 + preact * (1.0 - sig))
@@ -331,22 +378,25 @@
         h1_copy(a, peer).start()
     hall[b, pl.ds(pl.multiple_of((a + 1) * cols, 32), cols)] = hpack[a]
 
-    @pl.when(b > 0)
+    @pl.when(not_last)
+    def _():
+        to_earlier().wait_recv()
+
+    @pl.when(not_last & not_top)
+    def _():
+        next_above().start()
+
+    @pl.when(not_last & not_bottom)
+    def _():
+        next_below().start()
+
+    @pl.when(not_top)
     def _():
         to_below().wait_recv()
 
-    @pl.when(b < nr - 1)
+    @pl.when(not_bottom)
     def _():
         to_above().wait_recv()
-
-    def to_earlier():
-        return to_tm(
-            ext.at[:, pl.ds(0, pos)], ext.at[:, pl.ds(pos, pos)], ha_s.at[2], ha_r.at[2], lax.rem(a + nt - 1, nt)
-        )
-
-    @pl.when(a > 0)
-    def _():
-        to_earlier().start()
 
     w_copy.wait()
 
@@ -362,21 +412,28 @@
 
     lax.fori_loop(0, 3, dense_own, 0)
 
+    for peer in line_peers:
+        u2_copy(peer, peer).wait_recv()
+        u3_copy(peer).start()
+
+    def pass_on(row, src, ssem, rsem, peer):
+        place = hall.at[row, pl.ds((src + 1) * cols, cols)]
+        return to_row(place, place, ssem.at[src], rsem.at[src], peer)
+
+    pass_on(b, a, hy_s, hy_r, across).start()
+    pass_on(b, a, hc_s, hc_r, twin).start()
     for peer in tm_peers:
         h1_copy(peer, peer).wait_recv()
-
-    def h2_copy(src, peer):
-        place = pl.ds(cols, nt * cols)
-        return to_row(
-            hall.at[src, place], hall.at[src, place], h2_s.at[peer], h2_r.at[src], peer
-        )
-
-    for peer in row_peers:
-        h2_copy(b, peer).start()
-
-    @pl.when(a < nt - 1)
-    def _():
-        to_earlier().wait_recv()
+        pass_on(b, peer, hy_s, hy_r, across).start()
+        pass_on(b, peer, hc_s, hc_r, twin).start()
+
+    @pl.when(not_last & not_top)
+    def _():
+        next_below().wait_recv()
+
+    @pl.when(not_last & not_bottom)
+    def _():
+        next_above().wait_recv()
 
     def dense_rest(c, carry):
         val = acc[c]
@@ -401,7 +458,10 @@
 
         lax.fori_loop(0, 3, dense_first, 0)
 
-    sg_r[b, 2:8] = jnp.zeros((6, chans), F32)
+    for src in [a] + tm_peers:
+        pass_on(across, src, hy_s, hy_r, across).wait_recv()
+        pass_on(across, src, hf_s, hf_r, twin).start()
+
     for q in range(chans // 128):
         lanes = slice(q * 128, q * 128 + 128)
         sum_gain = jnp.zeros((1, 128), F32)
@@ -417,13 +477,13 @@
             dact_s[rows, lanes] = act
             sum_gain = sum_gain + jnp.sum(act * normed_s[rows, lanes], axis=0, keepdims=True)
             sum_bias = sum_bias + jnp.sum(act, axis=0, keepdims=True)
-        sg_r[b, 0:1, lanes] = sum_gain
-        sg_r[b, 1:2, lanes] = sum_bias
+        sg_r[b, q : q + 1] = sum_gain
+        sg_r[b, nq + q : nq + q + 1] = sum_bias
     for peer in row_peers:
         to_row(sg_r.at[b], sg_r.at[b], sg_rs.at[peer], sg_rr.at[b], peer).start()
 
-    for peer in tm_peers:
-        u2_copy(peer, peer).wait_recv()
+    for src in [side] + [lax.rem(side + d, nt) for d in range(2, nt, 2)]:
+        u3_copy(src).wait_recv()
     half = nt * cols // 2
     for part_index in range(2):
         rows = slice(part_index * half, part_index * half + half)
@@ -449,8 +509,9 @@
     for peer in tm_peers:
         to_tm(sg_t.at[a], sg_t.at[a], sg_ts.at[peer], sg_tr.at[a], peer).start()
 
-    for peer in row_peers:
-        h2_copy(peer, peer).wait_recv()
+    for src in [a] + tm_peers:
+        pass_on(twin, src, hc_s, hc_r, twin).wait_recv()
+        pass_on(far, src, hf_s, hf_r, twin).wait_recv()
     low = lax.broadcasted_iota(jnp.int32, (cols, 128), 1) < 64
     for r in range(nr):
         block = hall[r, cols : 2 * cols].astype(F32)
@@ -478,44 +539,54 @@
     total = sg_t[0]
     for t in range(1, nt):
         total = total + sg_t[t]
-    gg_ref[...] = total[0:1]
-    gb_ref[...] = total[1:2]
-    terms = group_total(total * gain, group_size) / count
-    second_term = terms[0:1]
-    first_term = terms[1:2]
-    for q in range(chans // 128):
+    for q in range(nq):
         lanes = slice(q * 128, q * 128 + 128)
+        gain = gain_ref[:, lanes]
+        gg_ref[:, lanes] = total[q : q + 1]
+        gb_ref[:, lanes] = total[nq + q : nq + q + 1]
+        second_term = group_total(total[q : q + 1] * gain, group_size) / count
+        first_term = group_total(total[nq + q : nq + q + 1] * gain, group_size) / count
         gf_ref[:, lanes] = (
-            inverse[:, lanes]
-            * (
-                dact_s[:, lanes] * gain[:, lanes]
-                - first_term[:, lanes]
-                - normed_s[:, lanes] * second_term[:, lanes]
-            )
+            inverse[q : q + 1]
+            * (dact_s[:, lanes] * gain - first_term - normed_s[:, lanes] * second_term)
         ).astype(BF16)
 
     for peer in row_peers:
         to_row(st_r.at[b], st_r.at[b], st_rs.at[peer], st_rr.at[b], peer).wait_send()
         to_row(sg_r.at[b], sg_r.at[b], sg_rs.at[peer], sg_rr.at[b], peer).wait_send()
         u1_copy(b, peer).wait_send()
-        h2_copy(b, peer).wait_send()
     for peer in tm_peers:
         to_tm(st_t.at[a], st_t.at[a], st_ts.at[peer], st_tr.at[a], peer).wait_send()
         to_tm(sg_t.at[a], sg_t.at[a], sg_ts.at[peer], sg_tr.at[a], peer).wait_send()
+        h1_copy(a, peer).wait_send()
+    u3_copy(a).wait_send()
+    for peer in line_peers:
         u2_copy(a, peer).wait_send()
-        h1_copy(a, peer).wait_send()
-
-    @pl.when(b > 0)
+        u3_copy(peer).wait_send()
+    for src in [a] + tm_peers:
+        pass_on(b, src, hy_s, hy_r, across).wait_send()
+        pass_on(b, src, hc_s, hc_r, twin).wait_send()
+        pass_on(across, src, hf_s, hf_r, twin).wait_send()
+
+    @pl.when(not_top)
     def _():
         to_above().wait_send()
 
-    @pl.when(b < nr - 1)
+    @pl.when(not_bottom)
     def _():
         to_below().wait_send()
 
-    @pl.when(a > 0)
+    @pl.when(not_first)
     def _():
         to_earlier().wait_send()
+
+    @pl.when(not_last & not_top)
+    def _():
+        next_above().wait_send()
+
+    @pl.when(not_last & not_bottom)
+    def _():
+        next_below().wait_send()
 
 
 def fused(features, norm_gain, norm_bias, weight, upstream):
@@ -535,9 +606,13 @@
             jax.ShapeDtypeStruct((1, chans), F32),
             jax.ShapeDtypeStruct((1, chans), F32),
         ),
-        in_specs=[vmem, vmem, vmem, pl.BlockSpec(memory_space=pl.ANY), vmem],
+        in_specs=[pl.BlockSpec(memory_space=pltpu.HBM)] * 5,
         out_specs=(vmem, vmem, vmem, vmem),
         scratch_shapes=[
+            pltpu.VMEM((pos, chans), BF16),
+            pltpu.VMEM((1, chans), F32),
+            pltpu.VMEM((1, chans), F32),
+            pltpu.VMEM((pos, outs), BF16),
             pltpu.VMEM((3, 3, 3, chans, outs), BF16),
             pltpu.VMEM((3, 2 * pos, outs), BF16),
             pltpu.VMEM((3, pos, chans), F32),
@@ -549,16 +624,17 @@
             pltpu.VMEM((nr, span, 128), BF16),
             pltpu.VMEM((nr, 384, span), BF16),
             pltpu.VMEM((3, 384, 256), F32),
-            pltpu.VMEM((nr, 8, chans), F32),
-            pltpu.VMEM((nt, 8, chans), F32),
-            pltpu.VMEM((nr, 8, chans), F32),
-            pltpu.VMEM((nt, 8, chans), F32),
-            dma,
+            pltpu.VMEM((nr, 8, 128), F32),
+            pltpu.VMEM((nt, 8, 128), F32),
+            pltpu.VMEM((nr, 8, 128), F32),
+            pltpu.VMEM((nt, 8, 128), F32),
+            dma((5,)),
             dma((nr,)), dma((nr,)), dma((nt,)), dma((nt,)),
             dma((nr,)), dma((nr,)), dma((nt,)), dma((nt,)),
-            dma((3,)), dma((3,)),
-            dma((nr,)), dma((nr,)), dma((nt,)), dma((nt,)),
-            dma((nt,)), dma((nt,)), dma((nr,)), dma((nr,)),
+            dma((5,)), dma((5,)),
+            dma((nr,)), dma((nr,)), dma((nt,)), dma((nt,)), dma((nt,)),
+            dma((nt,)), dma((nt,)), dma((nt,)), dma((nt,)),
+            dma((nt,)), dma((nt,)), dma((nt,)), dma((nt,)),
         ],
         compiler_params=pltpu.CompilerParams(
             collective_id=0, has_side_effects=True, vmem_limit_bytes=48 * 1024 * 1024
@@ -585,6 +661,7 @@
     fits = (
         CLIPS == 1
         and (frames_dev, rows_dev) == (2, 1)
+        and (nt, nr) == (8, 4)
         and (chans, outs) == (64 * nt, 64 * nr)
         and cols % 32 == 0
         and (nt * cols) % 256 == 0

time: 79.6 us -> 56.6 us (0.71)
  Pallas kernels: 72.7 us -> 49.7 us
    pallas_call x1, Pallas kernels: 72.7 us -> 49.7 us  [fused(): pl.pallas_call(functools.partial(kernel, dims), out_shape=(jax.ShapeDtype...]
where the time goes in v2:
time: 56.6 us; the launch traced here: 56.4 us
  Pallas kernels  49.7 us (88%)
  local copies, waits for them, and re-layouts  6.04 us (11%)
  between operations  0.65 us (1%)
    pallas_call x1, Pallas kernels, fused(): pl.pallas_call(functools.partial(kernel, dims), out_shape=(jax.ShapeDtype...  49.7 us
    unnamed x12, local copies, waits for them, and re-layouts  6.04 us

profile of v2, /device:TPU:0, one launch (start us, length us, event | category | flops | bytes accessed | tf_op | source)
XLA Modules:
  0.0 56.4 jit_solution(13017566260725115119)
XLA Ops:
  0.6 0.0 copy-start
  0.6 1.0 %copy-done = bf16[2,1,160,512]{3,2,1,0:T(8,128)(2,1)S(1)} copy-done((bf16[2,1,160,512]{3,2,1,0:T(8,128)(2,1)S(1)}, bf16[2,1,160,512]{3,2,1,0:T(8,128)(2,1)}, u32[]{:S(2)}) %copy-start) | copy-done | bytes 327704
  1.6 0.0 copy-start.1
  1.6 0.9 %copy-done.1 = bf16[2,1,160,256]{3,2,1,0:T(8,128)(2,1)S(1)} copy-done((bf16[2,1,160,256]{3,2,1,0:T(8,128)(2,1)S(1)}, bf16[2,1,160,256]{3,2,1,0:T(8,128)(2,1)}, u32[]{:S(2)}) %copy-start.1) | copy-done | bytes 163864
  2.5 0.0 copy-start.2
  2.5 0.7 %copy-done.2 = f32[512]{0:T(512)S(1)} copy-done((f32[512]{0:T(512)S(1)}, f32[512]{0:T(512)}, u32[]{:S(2)}) %copy-start.2) | copy-done | bytes 2072
  3.2 0.0 copy-start.3
  3.2 0.7 %copy-done.3 = f32[512]{0:T(512)S(1)} copy-done((f32[512]{0:T(512)S(1)}, f32[512]{0:T(512)}, u32[]{:S(2)}) %copy-start.3) | copy-done | bytes 2072
  3.9 49.7 %shard_map.84 = (bf16[320,512]{1,0:T(8,128)(2,1)S(1)}, f32[27,64,64]{2,1,0:T(8,128)S(1)}, f32[1,512]{1,0:T(1,128)S(1)}, f32[1,512]{1,0:T(1,128)S(1)}) custom-call(bf16[320,512]{1,0:T(8,128)(2,1)S(1)} %bitcast.11, f32[1,512]{1,0:T(1,128)S(1)} %bitcast.14, f32[1,512]{1,0:T(1,128)S(1)} %bitcast.15, bf16[3,3,3,512,256]{4,3,2,1,0:T(8,128)(2,1)} %weight_hbm.1, ...), custom_call_target="tpu_custom_call" | custom-call | tf_op jit(solution)/shard_map/pallas_call | solution.py:601
  53.6 0.7 %copy.14 = bf16[2,1,160,512]{3,2,1,0:T(8,128)(2,1)} copy(bf16[2,1,160,512]{3,2,1,0:T(8,128)(2,1)S(1)} %bitcast.12) | data formatting | bytes 655360
  54.3 0.9 %copy.15 = f32[3,3,3,64,64]{4,3,2,1,0:T(8,128)} copy(f32[3,3,3,64,64]{4,3,2,1,0:T(8,128)S(1)} %bitcast.10) | data formatting | bytes 884736
  55.2 0.6 %copy.16 = f32[512]{0:T(512)} copy(f32[512]{0:T(512)S(1)} %bitcast.17) | data formatting | bytes 4096
  55.8 0.6 %copy.17 = f32[512]{0:T(512)} copy(f32[512]{0:T(512)S(1)} %bitcast.16) | data formatting | bytes 4096
Async XLA Ops:
  0.6 1.0 %copy-start = (bf16[2,1,160,512]{3,2,1,0:T(8,128)(2,1)S(1)}, bf16[2,1,160,512]{3,2,1,0:T(8,128)(2,1)}, u32[]{:S(2)}) copy-start(bf16[2,1,160,512]{3,2,1,0:T(8,128)(2,1)} %param.5) | copy-start | bytes 983044
  1.6 0.9 %copy-start.1 = (bf16[2,1,160,256]{3,2,1,0:T(8,128)(2,1)S(1)}, bf16[2,1,160,256]{3,2,1,0:T(8,128)(2,1)}, u32[]{:S(2)}) copy-start(bf16[2,1,160,256]{3,2,1,0:T(8,128)(2,1)} %param.9) | copy-start | bytes 491524
  2.5 0.7 %copy-start.2 = (f32[512]{0:T(512)S(1)}, f32[512]{0:T(512)}, u32[]{:S(2)}) copy-start(f32[512]{0:T(512)} %param.6) | copy-start | bytes 6148
  3.2 0.7 %copy-start.3 = (f32[512]{0:T(512)S(1)}, f32[512]{0:T(512)}, u32[]{:S(2)}) copy-start(f32[512]{0:T(512)} %param.7) | copy-start | bytes 6148

commit v3 on v2

--- a/solution.py
+++ b/solution.py
@@ -327,10 +327,10 @@
     for peer in row_peers:
         u1_copy(peer, peer).wait_recv()
 
-    def u2_copy(src, peer):
+    def u2_copy(src, peer, ssem):
         place = pl.ds(src * cols, cols)
         return to_tm(
-            uall.at[:, place], uall.at[:, place], u2_s.at[peer], u2_r.at[src], peer
+            uall.at[:, place], uall.at[:, place], ssem, u2_r.at[src], peer
         )
 
     def u3_copy(src):
@@ -339,8 +339,14 @@
             uall.at[:, place], uall.at[:, place], u3_s.at[src], u2_r.at[src], side
         )
 
-    for peer in line_peers:
-        u2_copy(a, peer).start()
+    @pl.when(a + 2 < nt)
+    def _():
+        u2_copy(a, lax.rem(a + 2, nt), u2_s.at[a]).start()
+
+    @pl.when(a >= 2)
+    def _():
+        u2_copy(a, lax.rem(a + nt - 2, nt), u2_s.at[side]).start()
+
     u3_copy(a).start()
 
     for peer in tm_peers:
@@ -412,9 +418,6 @@
 
     lax.fori_loop(0, 3, dense_own, 0)
 
-    for peer in line_peers:
-        u2_copy(peer, peer).wait_recv()
-        u3_copy(peer).start()
 
     def pass_on(row, src, ssem, rsem, peer):
         place = hall.at[row, pl.ds((src + 1) * cols, cols)]
@@ -426,6 +429,29 @@
         h1_copy(peer, peer).wait_recv()
         pass_on(b, peer, hy_s, hy_r, across).start()
         pass_on(b, peer, hc_s, hc_r, twin).start()
+
+    for d in range(1, nt // 2):
+        src_low, src_high = a - 2 * d, a + 2 * d
+
+        @pl.when(src_low >= 0)
+        def _(src=src_low):
+            u2_copy(src, a, u2_s.at[a]).wait_recv()
+
+            @pl.when(a + 2 < nt)
+            def _():
+                u2_copy(src, lax.rem(a + 2, nt), u2_s.at[src]).start()
+
+            u3_copy(src).start()
+
+        @pl.when(src_high < nt)
+        def _(src=src_high):
+            u2_copy(src, a, u2_s.at[a]).wait_recv()
+
+            @pl.when(a >= 2)
+            def _():
+                u2_copy(src, lax.rem(a + nt - 2, nt), u2_s.at[src]).start()
+
+            u3_copy(src).start()
 
     @pl.when(not_last & not_top)
     def _():
@@ -561,8 +587,24 @@
         h1_copy(a, peer).wait_send()
     u3_copy(a).wait_send()
     for peer in line_peers:
-        u2_copy(a, peer).wait_send()
         u3_copy(peer).wait_send()
+
+    @pl.when(a + 2 < nt)
+    def _():
+        u2_copy(a, lax.rem(a + 2, nt), u2_s.at[a]).wait_send()
+
+    @pl.when(a >= 2)
+    def _():
+        u2_copy(a, lax.rem(a + nt - 2, nt), u2_s.at[side]).wait_send()
+
+    for d in range(1, nt // 2):
+        @pl.when((a - 2 * d >= 0) & (a + 2 < nt))
+        def _(src=a - 2 * d):
+            u2_copy(src, lax.rem(a + 2, nt), u2_s.at[src]).wait_send()
+
+        @pl.when((a + 2 * d < nt) & (a >= 2))
+        def _(src=a + 2 * d):
+            u2_copy(src, lax.rem(a + nt - 2, nt), u2_s.at[src]).wait_send()
     for src in [a] + tm_peers:
         pass_on(b, src, hy_s, hy_r, across).wait_send()
         pass_on(b, src, hc_s, hc_r, twin).wait_send()

time: 56.6 us -> 51.3 us (0.906)
  Pallas kernels: 49.7 us -> 44.4 us
    pallas_call x1, Pallas kernels: 49.7 us -> 44.4 us  [fused(): pl.pallas_call(functools.partial(kernel, dims), out_shape=(jax.ShapeDtype...]
where the time goes in v3:
time: 51.3 us; the launch traced here: 51 us
  Pallas kernels  44.4 us (87%)
  local copies, waits for them, and re-layouts  6.04 us (12%)
  between operations  0.65 us (1%)
    pallas_call x1, Pallas kernels, fused(): pl.pallas_call(functools.partial(kernel, dims), out_shape=(jax.ShapeDtype...  44.4 us
    unnamed x12, local copies, waits for them, and re-layouts  6.04 us

profile of v3, /device:TPU:0, one launch (start us, length us, event | category | flops | bytes accessed | tf_op | source)
XLA Modules:
  0.0 51.0 jit_solution(2069945962085110448)
XLA Ops:
  0.6 0.0 copy-start
  0.6 1.0 %copy-done = bf16[2,1,160,512]{3,2,1,0:T(8,128)(2,1)S(1)} copy-done((bf16[2,1,160,512]{3,2,1,0:T(8,128)(2,1)S(1)}, bf16[2,1,160,512]{3,2,1,0:T(8,128)(2,1)}, u32[]{:S(2)}) %copy-start) | copy-done | bytes 327704
  1.6 0.0 copy-start.1
  1.6 0.9 %copy-done.1 = bf16[2,1,160,256]{3,2,1,0:T(8,128)(2,1)S(1)} copy-done((bf16[2,1,160,256]{3,2,1,0:T(8,128)(2,1)S(1)}, bf16[2,1,160,256]{3,2,1,0:T(8,128)(2,1)}, u32[]{:S(2)}) %copy-start.1) | copy-done | bytes 163864
  2.5 0.0 copy-start.2
  2.5 0.7 %copy-done.2 = f32[512]{0:T(512)S(1)} copy-done((f32[512]{0:T(512)S(1)}, f32[512]{0:T(512)}, u32[]{:S(2)}) %copy-start.2) | copy-done | bytes 2072
  3.2 0.0 copy-start.3
  3.2 0.7 %copy-done.3 = f32[512]{0:T(512)S(1)} copy-done((f32[512]{0:T(512)S(1)}, f32[512]{0:T(512)}, u32[]{:S(2)}) %copy-start.3) | copy-done | bytes 2072
  3.9 44.4 %shard_map.84 = (bf16[320,512]{1,0:T(8,128)(2,1)S(1)}, f32[27,64,64]{2,1,0:T(8,128)S(1)}, f32[1,512]{1,0:T(1,128)S(1)}, f32[1,512]{1,0:T(1,128)S(1)}) custom-call(bf16[320,512]{1,0:T(8,128)(2,1)S(1)} %bitcast.11, f32[1,512]{1,0:T(1,128)S(1)} %bitcast.14, f32[1,512]{1,0:T(1,128)S(1)} %bitcast.15, bf16[3,3,3,512,256]{4,3,2,1,0:T(8,128)(2,1)} %weight_hbm.1, ...), custom_call_target="tpu_custom_call" | custom-call | tf_op jit(solution)/shard_map/pallas_call | solution.py:643
  48.3 0.7 %copy.14 = bf16[2,1,160,512]{3,2,1,0:T(8,128)(2,1)} copy(bf16[2,1,160,512]{3,2,1,0:T(8,128)(2,1)S(1)} %bitcast.12) | data formatting | bytes 655360
  49.0 0.9 %copy.15 = f32[3,3,3,64,64]{4,3,2,1,0:T(8,128)} copy(f32[3,3,3,64,64]{4,3,2,1,0:T(8,128)S(1)} %bitcast.10) | data formatting | bytes 884736
  49.9 0.6 %copy.16 = f32[512]{0:T(512)} copy(f32[512]{0:T(512)S(1)} %bitcast.17) | data formatting | bytes 4096
  50.5 0.6 %copy.17 = f32[512]{0:T(512)} copy(f32[512]{0:T(512)S(1)} %bitcast.16) | data formatting | bytes 4096
Async XLA Ops:
  0.6 1.0 %copy-start = (bf16[2,1,160,512]{3,2,1,0:T(8,128)(2,1)S(1)}, bf16[2,1,160,512]{3,2,1,0:T(8,128)(2,1)}, u32[]{:S(2)}) copy-start(bf16[2,1,160,512]{3,2,1,0:T(8,128)(2,1)} %param.5) | copy-start | bytes 983044
  1.6 0.9 %copy-start.1 = (bf16[2,1,160,256]{3,2,1,0:T(8,128)(2,1)S(1)}, bf16[2,1,160,256]{3,2,1,0:T(8,128)(2,1)}, u32[]{:S(2)}) copy-start(bf16[2,1,160,256]{3,2,1,0:T(8,128)(2,1)} %param.9) | copy-start | bytes 491524
  2.5 0.7 %copy-start.2 = (f32[512]{0:T(512)S(1)}, f32[512]{0:T(512)}, u32[]{:S(2)}) copy-start(f32[512]{0:T(512)} %param.6) | copy-start | bytes 6148
  3.2 0.7 %copy-start.3 = (f32[512]{0:T(512)S(1)}, f32[512]{0:T(512)}, u32[]{:S(2)}) copy-start(f32[512]{0:T(512)} %param.7) | copy-start | bytes 6148
